TPU v7x, 32 devices: a whole 2x2x4 slice. The times are simulated.
32 devices in a mesh: guide: 2 (over core), row: 4 (over z), col: 4 (over y, x).
Axes of the slice: x: 2, y: 2, z: 4, core: 2. Of those that a mesh axis runs over, the one named last changes fastest.
Arguments:
- hidden: bfloat16 [2, 16, 2048], P('guide', None, 'row')
- lengths: int32 [2, 16], P('guide'), may hold values from 2 to 512, as said below
- kv_cache: bfloat16 [2, 16, 2, 512, 512], P('guide', None, None, 'row', 'col'), as said below
- attn_gain: bfloat16 [2048], P('row'), may hold values from 0.5 to 1.5
- w_query: bfloat16 [2048, 2048], P('row', 'col'), may hold values from -0.125 to 0.125
- w_key_value: bfloat16 [2048, 2, 512], P('row', None, 'col'), may hold values from -0.125 to 0.125
- w_out: bfloat16 [2048, 2048], P('col', 'row'), may hold values from -0.125 to 0.125
- mlp_gain: bfloat16 [2048], P('row'), may hold values from 0.5 to 1.5
- w_gate_up: bfloat16 [2048, 2, 8192], P('row', None, 'col'), may hold values from -0.125 to 0.125
- w_down: bfloat16 [8192, 2048], P('col', 'row'), may hold values from -0.0625 to 0.0625
- final_gain: bfloat16 [2048], P('row'), may hold values from 0.5 to 1.5
- w_head: bfloat16 [2048, 128256], P('row', 'col'), may hold values from -0.1875 to 0.1875
- next_gain: bfloat16 [2048], P('row'), may hold values from 0.5 to 1.5
- w_next_query: bfloat16 [2048, 2048], P('row', 'col'), may hold values from -0.125 to 0.125
- w_next_kv: bfloat16 [2048, 2, 512], P('row', None, 'col'), may hold values from -0.125 to 0.125
- tenant: int32 [16], replicated, may hold values from 0 to 3
- guide_scale: float32 [4], replicated, may hold values from 1.5 to 6
Outputs:
- guided_logits: float32 [16, 128256], P('guide', ('col', 'row'))
- next_query: bfloat16 [2, 16, 2048], P('guide', None, 'col')
- next_key_value: bfloat16 [2, 16, 2, 512], P('guide', None, None, 'col')
Inputs may be any that keep to these rules, and one draw needn't show every extreme that they name: `lengths`: in each group one request has exactly 512 cached positions. `kv_cache`: keys (index 0 of the third dimension) are stored with the rotary embedding of their positions; values at index 1.
All inputs are finite; a program needn't handle non-finite values.
Results may differ from a plain program's by a relative error of at most 0.013.
Values may be sent and summed in bfloat16 or wider, within the bound.
A program may use at most 128 MiB of HBM per device.

v0:
```python
import jax
import jax.numpy as jnp
from jax import lax
from jax.sharding import PartitionSpec as P

D = 2048
HEADS = 32
KVH = 8
HD = 64
TENANTS = 4


EPSILON = 1e-05
ROPE_BASE = 500000.0
NEGATIVE = -1e30


def joined(x, axis, combine):
    everything = jax.tree.map(lambda part: lax.all_gather(part, axis), x)
    first = jax.tree.map(lambda part: part[0], everything)

    def turn(k, so_far):
        return combine(so_far, jax.tree.map(lambda part: part[k], everything))

    return lax.fori_loop(1, lax.axis_size(axis), turn, first)


def partner_2(x, axis, apart):
    return lax.ppermute(x, axis, [(i, i ^ 1 << apart) for i in range(lax.axis_size(axis))])


def rotate(vectors, position):
    half_width = vectors.shape[-1] // 2
    frequency = ROPE_BASE ** (-2.0 * jnp.arange(half_width, dtype=jnp.float32) / vectors.shape[-1])
    angles = position.astype(jnp.float32)[:, None] * frequency[None, :]
    angles = angles.reshape((angles.shape[0],) + (1,) * (vectors.ndim - 2) + (half_width,))
    cosine = jnp.cos(angles)
    sines = jnp.sin(angles)
    first_half = vectors[..., :half_width]
    second_half = vectors[..., half_width:]
    return jnp.concatenate(
        [first_half * cosine - second_half * sines, second_half * cosine + first_half * sines],
        axis=-1,
    )


def squares(values):
    return jnp.sum(values * values, axis=1)


def join_parts(first, second):
    best_a, norm_a, weighted_a = first
    best_b, norm_b, weighted_b = second
    best = jnp.maximum(best_a, best_b)
    factor_a = jnp.exp(best_a - best)
    factor_b = jnp.exp(best_b - best)
    return (
        best,
        norm_a * factor_a + norm_b * factor_b,
        weighted_a * factor_a[..., None] + weighted_b * factor_b[..., None],
    )


def local(
    hidden,
    lengths,
    kv_cache,
    attn_gain,
    w_query,
    w_key_value,
    w_out,
    mlp_gain,
    w_gate_up,
    w_down,
    final_gain,
    w_head,
    next_gain,
    w_next_query,
    w_next_kv,
    tenant,
    guide_scale,
):
    x_rows = hidden[0]
    length = lengths[0]
    cache_block = kv_cache[0]
    requests = x_rows.shape[0]
    local_width = x_rows.shape[1]
    group_size = HEADS // KVH
    heads_here = w_key_value.shape[2] // HD
    x_float = x_rows.astype(jnp.float32)
    normed = (x_float * attn_gain.astype(jnp.float32)).astype(jnp.bfloat16)
    query_part = jnp.dot(normed, w_query, preferred_element_type=jnp.float32)
    pair_part = jnp.dot(
        normed, w_key_value.reshape(local_width, -1), preferred_element_type=jnp.float32
    )
    query_sum, pair_sum, first_squares = lax.psum((query_part, pair_part, squares(x_float)), "row")
    scaling = lax.rsqrt(first_squares / D + EPSILON)[:, None]
    query = rotate(
        (scaling * query_sum).reshape(requests, heads_here, group_size, HD), length
    ).astype(jnp.bfloat16)
    key_value = (scaling * pair_sum).reshape(requests, 2, heads_here, HD)
    new_key = rotate(key_value[:, 0], length).astype(jnp.bfloat16)
    new_value = key_value[:, 1].astype(jnp.bfloat16)
    cache_span = cache_block.shape[2]
    cache_keys = cache_block[:, 0].reshape(requests, cache_span, heads_here, HD)
    cache_values = cache_block[:, 1].reshape(requests, cache_span, heads_here, HD)
    inv_scale = HD ** (-0.5)
    scores = (
        jnp.einsum("bhgd,bshd->bhgs", query, cache_keys, preferred_element_type=jnp.float32)
        * inv_scale
    )
    positions = lax.axis_index("row") * cache_span + jnp.arange(cache_span, dtype=jnp.int32)
    usable = (positions[None, :] < length[:, None])[:, None, None, :]
    masked = jnp.where(usable, scores, NEGATIVE)
    local_best = jnp.max(masked, axis=-1)
    exp_terms = jnp.where(usable, jnp.exp(masked - local_best[..., None]), 0.0)
    local_norm = jnp.sum(exp_terms, axis=-1)
    local_weighted = jnp.einsum(
        "bhgs,bshd->bhgd",
        exp_terms.astype(jnp.bfloat16),
        cache_values,
        preferred_element_type=jnp.float32,
    )
    best, norm_sum, weighted = joined((local_best, local_norm, local_weighted), "row", join_parts)
    own_score = (
        jnp.einsum("bhgd,bhd->bhg", query, new_key, preferred_element_type=jnp.float32) * inv_scale
    )
    final_best = jnp.maximum(best, own_score)
    rescale = jnp.exp(best - final_best)
    own_exp = jnp.exp(own_score - final_best)
    norm_sum = norm_sum * rescale + own_exp
    weighted = weighted * rescale[..., None] + jnp.einsum(
        "bhg,bhd->bhgd", own_exp.astype(jnp.bfloat16), new_value, preferred_element_type=jnp.float32
    )
    attended = (weighted / norm_sum[..., None]).reshape(requests, -1).astype(jnp.bfloat16)
    out_part = jnp.dot(attended, w_out, preferred_element_type=jnp.float32)
    residual_one = (x_float + lax.psum(out_part, "col")).astype(jnp.bfloat16)
    one_float = residual_one.astype(jnp.float32)
    mlp_input = (one_float * mlp_gain.astype(jnp.float32)).astype(jnp.bfloat16)
    gate_part = jnp.dot(
        mlp_input, w_gate_up.reshape(local_width, -1), preferred_element_type=jnp.float32
    ).reshape(requests, 2, -1)
    gate_up, second_squares = lax.psum((gate_part, squares(one_float)), "row")
    mlp_scale = lax.rsqrt(second_squares / D + EPSILON)[:, None]
    activation = (jax.nn.silu(mlp_scale * gate_up[:, 0]) * (mlp_scale * gate_up[:, 1])).astype(
        jnp.bfloat16
    )
    down_part = jnp.dot(activation, w_down, preferred_element_type=jnp.float32)
    residual_two = (one_float + lax.psum(down_part, "col")).astype(jnp.bfloat16)
    two_float = residual_two.astype(jnp.float32)
    head_input = (two_float * final_gain.astype(jnp.float32)).astype(jnp.bfloat16)
    next_input = (two_float * next_gain.astype(jnp.float32)).astype(jnp.bfloat16)
    next_query_part = jnp.dot(next_input, w_next_query, preferred_element_type=jnp.float32)
    next_pair_part = jnp.dot(
        next_input, w_next_kv.reshape(local_width, -1), preferred_element_type=jnp.float32
    )
    next_query_sum, next_pair_sum, third_squares = lax.psum(
        (next_query_part, next_pair_part, squares(two_float)), "row"
    )
    out_scale = lax.rsqrt(third_squares / D + EPSILON)[:, None]
    next_query = (out_scale * next_query_sum).astype(jnp.bfloat16)[None]
    next_key_value = (out_scale * next_pair_sum).astype(jnp.bfloat16).reshape(1, requests, 2, -1)
    head_part = jnp.dot(head_input, w_head, preferred_element_type=jnp.float32)
    guidance = jnp.sum(
        jnp.where(
            tenant[:, None] == jnp.arange(TENANTS, dtype=jnp.int32)[None, :],
            guide_scale[None, :],
            0.0,
        ),
        axis=1,
    )
    guide_side = lax.axis_index("guide")
    half_rows = requests // 2
    own_logits = out_scale * lax.psum_scatter(head_part, "row", scatter_dimension=1, tiled=True)
    mine = lax.dynamic_slice_in_dim(own_logits, guide_side * half_rows, half_rows, 0)
    outgoing = lax.dynamic_slice_in_dim(own_logits, (1 - guide_side) * half_rows, half_rows, 0)
    partner = partner_2(outgoing, "guide", 0)
    conditional = jnp.where(guide_side == 0, mine, partner)
    unconditional = jnp.where(guide_side == 0, partner, mine)
    my_guidance = lax.dynamic_slice_in_dim(guidance, guide_side * half_rows, half_rows, 0)
    guided = unconditional + my_guidance[:, None] * (conditional - unconditional)
    return (guided, next_query, next_key_value)


def solution(mesh):
    placed = (
        P("guide", None, "row"),
        P("guide", None),
        P("guide", None, None, "row", "col"),
        P("row"),
        P("row", "col"),
        P("row", None, "col"),
        P("col", "row"),
        P("row"),
        P("row", None, "col"),
        P("col", "row"),
        P("row"),
        P("row", "col"),
        P("row"),
        P("row", "col"),
        P("row", None, "col"),
        P(),
        P(),
    )
    return jax.shard_map(
        local,
        mesh=mesh,
        in_specs=placed,
        out_specs=(
            P("guide", ("col", "row")),
            P("guide", None, "col"),
            P("guide", None, None, "col"),
        ),
        check_vma=False,
    )
```

profile of v0, /device:TPU:9, one launch (start us, length us, event | category | flops | bytes accessed | tf_op | source)
XLA Modules:
  0.0 470.6 jit_solution(12770321997113881854)
XLA Ops:
  7.2 0.8 convert_element_type.85
  8.1 0.8 fusion.24
  8.9 1.2 fusion.46
  10.1 1.1 fusion.7
  11.3 13.0 %all-reduce.1 = (f32[16,512]{1,0:T(8,128)S(1)}, f32[16]{0:T(128)S(1)}, f32[16,256]{1,0:T(8,128)S(1)}) all-reduce(f32[16,512]{1,0:T(8,128)S(1)} %fusion.46, f32[16]{0:T(128)S(1)} %fusion.24, f32[16,256]{1,0:T(8,128)S(1)} %fusion.7), channel_id=1, replica_groups=mesh['guide'=2,'row'=4,'col'=4] {'row'}, use_global_device_ids=true, to_apply=%region_2.0 | all-reduce | flops 12304 | bytes 98432 | tf_op jit(solution)/shard_map/psum | solution.py:96
  24.5 6.6 %copy.77 = bf16[64,8,2,2048]{3,1,2,0:T(8,128)(2,1)} copy(bf16[64,8,2,2048]{3,2,1,0:T(2,128)(2,1)} %bitcast.115) | data formatting | bytes 8388608
  31.1 6.5 %copy.67 = bf16[4096,512]{1,0:T(8,128)(2,1)} copy(bf16[4096,512]{0,1:T(8,128)(2,1)} %bitcast.114) | data formatting | bytes 8388608 | tf_op jit(solution)/shard_map/dot_general | solution.py:140
  37.5 2.1 fusion.66
  39.6 1.3 copy.56
  41.9 10.2 %all-gather = f32[64,2,4]{2,1,0:T(2,128)S(1)} all-gather(f32[16,2,4]{2,1,0:T(2,128)S(1)} %get-tuple-element.244), channel_id=2, replica_groups=mesh['guide'=2,'row'=4,'col'=4] {'row'}, dimensions={0}, use_global_device_ids=true | all-gather | bytes 2560 | tf_op jit(solution)/shard_map/all_gather | solution.py:19
  52.4 10.4 %all-gather.1 = f32[64,2,4]{2,1,0:T(2,128)S(1)} all-gather(f32[16,2,4]{2,1,0:T(2,128)S(1)} %fusion.20), channel_id=3, replica_groups=mesh['guide'=2,'row'=4,'col'=4] {'row'}, dimensions={0}, use_global_device_ids=true | all-gather | bytes 2560 | tf_op jit(solution)/shard_map/all_gather | solution.py:19
  63.7 11.2 %all-gather.2 = f32[64,2,4,64]{3,2,1,0:T(4,128)S(1)} all-gather(f32[16,2,4,64]{3,2,1,0:T(4,128)S(1)} %fusion.28), channel_id=4, replica_groups=mesh['guide'=2,'row'=4,'col'=4] {'row'}, dimensions={0}, use_global_device_ids=true | all-gather | bytes 163840 | tf_op jit(solution)/shard_map/all_gather | solution.py:19
  75.1 1.4 while.19
  77.6 1.2 fusion.68
  78.9 12.5 %psum.73 = f32[16,512]{1,0:T(8,128)S(1)} all-reduce(f32[16,512]{1,0:T(8,128)S(1)} %fusion.68), channel_id=1, replica_groups=mesh['guide'=2,'row'=4,'col'=4] {'col'}, use_global_device_ids=true, to_apply=%region_8.9 | all-reduce | flops 8192 | bytes 65536 | tf_op jit(solution)/shard_map/psum | solution.py:137
  91.5 4.1 fusion.42
  95.7 10.0 %psum.74 = f32[16]{0:T(128)S(1)} all-reduce(f32[16]{0:T(128)S(1)} %get-tuple-element.231), channel_id=1, replica_groups=mesh['guide'=2,'row'=4,'col'=4] {'row'}, use_global_device_ids=true, to_apply=%region_10.11 | all-reduce | flops 16 | bytes 128 | tf_op jit(solution)/shard_map/psum | solution.py:143
  105.7 39.5 %all-reduce.4.cloned.1.call-done = f32[16,2,2048]{2,0,1:T(8,128)} async-done(((f32[16,2,2048]{2,0,1:T(8,128)}), f32[16,2,2048]{2,0,1:T(8,128)}) %all-reduce.4.cloned.1.call-update) | async-done | bytes 262160 | tf_op jit(solution)/shard_map/psum | solution.py:143
  145.3 1.4 fusion.14
  146.7 12.5 %psum.76 = f32[16,512]{1,0:T(8,128)S(1)} all-reduce(f32[16,512]{1,0:T(8,128)S(1)} %fusion.14), channel_id=1, replica_groups=mesh['guide'=2,'row'=4,'col'=4] {'col'}, use_global_device_ids=true, to_apply=%region_12.13 | all-reduce | flops 8192 | bytes 65536 | tf_op jit(solution)/shard_map/psum | solution.py:149
  159.3 20.5 %convolution_bitcast_fusion = f32[32064,16]{1,0:T(8,128)} fusion(bf16[512,32064]{0,1:T(8,128)(2,1)} %param.30, bf16[16,512]{1,0:T(8,128)(2,1)S(1)} %get-tuple-element.230, f32[512]{0:T(512)S(1)} %convert_element_type.102), kind=kOutput, calls=%fused_computation.8 | convolution fusion | flops 525361152 | bytes 34904064
  181.2 12.1 %all-reduce = (f32[16]{0:T(128)S(1)}, f32[16,512]{1,0:T(8,128)S(1)}, f32[16,256]{1,0:T(8,128)S(1)}) all-reduce(f32[16]{0:T(128)S(1)} %get-tuple-element.229, f32[16,512]{1,0:T(8,128)S(1)} %fusion.55, f32[16,256]{1,0:T(8,128)S(1)} %fusion.4), channel_id=1, replica_groups=mesh['guide'=2,'row'=4,'col'=4] {'row'}, use_global_device_ids=true, to_apply=%region_14.15 | all-reduce | flops 12304 | bytes 98432 | tf_op jit(solution)/shard_map/psum | solution.py:157
  193.3 264.7 %reduce-scatter.4.cloned.1.call-done = f32[8016,16]{1,0:T(8,128)} async-done(((f32[32064,16]{1,0:T(8,128)}), f32[8016,16]{1,0:T(8,128)}) %reduce-scatter.4.cloned.1.call-update) | async-done | bytes 513040
  458.0 3.0 copy.75
  (91 shorter events, 9.3 us)
Async XLA Ops:
  7.2 138.1 %copy-start = (bf16[2048,512]{1,0:T(8,128)(2,1)S(1)}, bf16[2048,512]{1,0:T(8,128)(2,1)}, u32[]{:S(2)}) copy-start(bf16[2048,512]{1,0:T(8,128)(2,1)} %param.28) | copy-start | bytes 6291460
  7.2 138.1 %all-reduce.4.cloned.1.call-start = ((), (), s32[]{:S(2)}) async-start(), calls=%async_computation.1 | async-start | bytes 524288 | tf_op jit(solution)/shard_map/psum | solution.py:143
  31.1 10.1 %copy-start.8 = (s32[1,16]{1,0:T(1,128)S(1)}, s32[1,16]{1,0:T(1,128)}, u32[]{:S(2)}) copy-start(s32[1,16]{1,0:T(1,128)} %param.20) | copy-start | bytes 196
  39.6 51.8 %copy-start.4 = (bf16[1,16,512]{2,1,0:T(8,128)(2,1)S(1)}, bf16[1,16,512]{2,1,0:T(8,128)(2,1)}, u32[]{:S(2)}) copy-start(bf16[1,16,512]{2,1,0:T(8,128)(2,1)} %param.19) | copy-start | bytes 49156
  39.6 51.9 %copy-start.5 = (bf16[512]{0:T(512)(128)(2,1)S(1)}, bf16[512]{0:T(512)(128)(2,1)}, u32[]{:S(2)}) copy-start(bf16[512]{0:T(512)(128)(2,1)} %param.26) | copy-start | bytes 3076
  63.7 32.1 %copy-start.6 = (bf16[512]{0:T(512)(128)(2,1)S(1)}, bf16[512]{0:T(512)(128)(2,1)}, u32[]{:S(2)}) copy-start(bf16[512]{0:T(512)(128)(2,1)} %param.29) | copy-start | bytes 3076
  95.7 362.3 %reduce-scatter.4.cloned.1.call-start = ((), (), s32[]{:S(2)}) async-start(), calls=%async_computation.2 | async-start | bytes 20520960
  179.8 0.7 copy-start.7
  179.8 0.7 copy-start.9
  179.8 0.7 copy-start.10
  179.8 1.0 copy-start.3
  179.8 1.2 copy-start.2
  179.9 283.9 %copy-start.1 = (bf16[2048,512]{1,0:T(8,128)(2,1)S(1)}, bf16[2048,512]{1,0:T(8,128)(2,1)}, u32[]{:S(2)}) copy-start(bf16[2048,512]{1,0:T(8,128)(2,1)} %param.28) | copy-start | bytes 6291460
  461.1 1.9 collective-permute-start
Sparse Core Ops, SparseCore 0:
  95.8 49.4 all-reduce.3
  180.0 277.9 reduce-scatter.3
where the time goes:
time: 473 us; the launch traced here: 471 us
  waiting for transfers between devices  304 us (64%)
  blocking collectives  92 us (19%)
  matrix products  31 us (7%)
  local copies, waits for them, and re-layouts  22.9 us (5%)
  between operations  14.3 us (3%)
  other arithmetic  5.49 us (1%)
    unnamed x3, waiting for transfers between devices  265 us
    psum x1, waiting for transfers between devices, local(): gate_up, second_squares = lax.psum((gate_part, squares(one_float)), 'row')  39.5 us
    all_gather x3, blocking collectives, joined(): everything = jax.tree.map(lambda part: lax.all_gather(part, axis), x)  31.9 us
    unnamed x1, matrix products  20.5 us
    psum x1, blocking collectives, local(): lax.psum((query_part, pair_part, squares(x_float)), 'row')  13 us
    psum x1, blocking collectives, local(): residual_one = (x_float + lax.psum(out_part, 'col')).astype(jnp.bfloat16)  12.5 us
    psum x1, blocking collectives, local(): residual_two = (one_float + lax.psum(down_part, 'col')).astype(jnp.bfloat16)  12.5 us
    psum x1, blocking collectives, local(): lax.psum((next_query_part, next_pair_part, squares(two_float)), 'row')  12.1 us
  transfers between devices with their start and end apart: 3, of which 2 were waited for; matrix products, arithmetic and copies ran while one was open for 0% of the time, Pallas kernels for 0%

commit v1 on v0

v1 whole, which is shorter than its diff:
```python
import functools
import math

import jax
import jax.numpy as jnp
from jax import lax
from jax.experimental import pallas as pl
from jax.experimental.pallas import tpu as pltpu
from jax.sharding import PartitionSpec as P

D = 2048
HEADS = 32
KVH = 8
HD = 64
TENANTS = 4
EPSILON = 1e-05
ROPE_BASE = 500000.0
NEGATIVE = -1e30
LANES = 128
SUBLANES = 16
F32 = jnp.float32
BF16 = jnp.bfloat16
MESH = pl.DeviceIdType.MESH


def mm(a, b):
    return jnp.dot(a, b, preferred_element_type=F32)


def iota(shape, dim):
    return lax.broadcasted_iota(jnp.int32, shape, dim)


def window_of(block):
    tiles = -(-(block + LANES - 1) // LANES)
    return (tiles + tiles % 2) * LANES


def layer_kernel(
    n,
    m,
    x_ref,
    len_ref,
    tenant_ref,
    guide_ref,
    gains_ref,
    kv_hbm,
    wq_hbm,
    wkv_hbm,
    wo_hbm,
    wgu_hbm,
    wd_hbm,
    wh_hbm,
    wnq_hbm,
    wnkv_hbm,
    out_ref,
    nq_ref,
    nkv_ref,
    kv,
    wq,
    wkv,
    wo,
    wgu,
    wd,
    wh,
    wnq,
    wnkv,
    q_buf,
    sq_buf,
    q_rows,
    a_buf,
    o_buf,
    sq2_buf,
    gu_send,
    gu_buf,
    act_buf,
    d_buf,
    two_buf,
    sq3_buf,
    np_buf,
    part,
    h_send,
    h_buf,
    local_sem,
    send_sem,
    recv_sem,
):
    row = lax.axis_index("row")
    col = lax.axis_index("col")
    guide = lax.axis_index("guide")
    place = {"row": (row, n), "col": (col, m), "guide": (guide, 2)}

    pairs = [
        (wq_hbm, wq),
        (wkv_hbm, wkv),
        (kv_hbm, kv),
        (wo_hbm, wo),
        (wgu_hbm, wgu),
        (wd_hbm, wd),
        (wnq_hbm, wnq),
        (wnkv_hbm, wnkv),
        (wh_hbm, wh),
    ]
    loads = [pltpu.make_async_copy(a, b, local_sem.at[i]) for i, (a, b) in enumerate(pairs)]
    for load in loads:
        load.start()

    def peer(axis, k):
        me, size = place[axis]
        return lax.rem(me + k, size)

    barrier = pltpu.get_barrier_semaphore()
    for axis in ("row", "col", "guide"):
        for k in range(1, place[axis][1]):
            pl.semaphore_signal(barrier, inc=1, device_id={axis: peer(axis, k)}, device_id_type=MESH)

    def send(source, target, axis, number, k):
        copy = pltpu.make_async_remote_copy(
            src_ref=source,
            dst_ref=target,
            send_sem=send_sem.at[number, k - 1],
            recv_sem=recv_sem.at[number, k - 1],
            device_id={axis: peer(axis, k)},
            device_id_type=MESH,
        )
        copy.start()
        return copy

    def spread(buf, axis, number):
        me, size = place[axis]
        return [send(buf.at[me], buf.at[me], axis, number, k) for k in range(1, size)]

    def finish(copies):
        for copy in copies:
            copy.wait()

    def total(buf, size):
        result = buf[0].astype(F32)
        for k in range(1, size):
            result = result + buf[k].astype(F32)
        return result

    def squares(values):
        return jnp.broadcast_to(jnp.sum(values * values, axis=1, keepdims=True), (values.shape[0], LANES))

    def scale_of(sums):
        return lax.rsqrt(sums / D + EPSILON)

    requests = x_ref.shape[0]
    half_rows = requests // 2
    x_float = x_ref[...].astype(F32)
    normed = (x_float * gains_ref[0:1, :]).astype(BF16)
    sq_buf[row] = squares(x_float)
    loads[0].wait()
    width_q = wq.shape[1]
    width_kv = wkv.shape[1]
    q_buf[row, :, 0:width_q] = mm(normed, wq[...]).astype(BF16)
    loads[1].wait()
    q_buf[row, :, width_q : width_q + width_kv] = mm(normed, wkv[...]).astype(BF16)
    pl.semaphore_wait(barrier, n - 1 + m - 1 + 1)
    copies = spread(sq_buf, "row", 0) + spread(q_buf, "row", 1)

    lane = iota((requests, LANES), 1)
    lengths_row = len_ref[...].astype(F32)
    pick = iota((requests, requests), 0) == iota((requests, requests), 1)
    length_col = jnp.sum(jnp.where(pick, lengths_row, 0.0), axis=1, keepdims=True)
    frequency = jnp.exp((lane % (HD // 2)).astype(F32) * (-2.0 * math.log(ROPE_BASE) / HD))
    angles = length_col * frequency
    cosine = jnp.cos(angles)
    sine = jnp.sin(angles)
    low = (lane % HD) < HD // 2
    signed = jnp.where(low, -sine, sine)
    left = lane < HD

    def rotated(tile):
        ahead = pltpu.roll(tile, LANES - HD // 2, 1)
        behind = pltpu.roll(tile, HD // 2, 1)
        return tile * cosine + jnp.where(low, ahead, behind) * signed

    finish(copies)
    scale = scale_of(total(sq_buf, n))
    sums = total(q_buf, n)
    tiles = [scale * sums[:, t * LANES : (t + 1) * LANES] for t in range((width_q + width_kv) // LANES)]
    q_tiles = width_q // LANES
    heads_here = 2 * q_tiles
    group = HEADS // KVH
    for t in range(q_tiles):
        tile = rotated(tiles[t]).astype(BF16).astype(F32)
        swapped = pltpu.roll(tile, HD, 1)
        for side in range(2):
            j = 2 * t + side
            kv_head = j // group
            wanted = tile if side == kv_head else swapped
            q_rows[:, j, :] = jnp.where(left == (kv_head == 0), wanted, 0.0)
    new_key = rotated(tiles[q_tiles]).astype(BF16).astype(F32)
    new_value = tiles[q_tiles + 1].astype(BF16).astype(F32)

    loads[2].wait()
    inv_scale = HD**-0.5
    span = kv.shape[2]
    rows3 = (requests, heads_here, LANES)
    q3 = q_rows[...]
    scores = jnp.stack(
        [
            lax.dot_general(
                q3[b].astype(BF16), kv[b, 0], (((1,), (1,)), ((), ())), preferred_element_type=F32
            )
            for b in range(requests)
        ]
    ) * inv_scale
    own_score = jnp.sum(q3 * new_key[:, None, :], axis=2, keepdims=True) * inv_scale
    length3 = length_col[:, :, None]
    position = (row * span + iota((requests, heads_here, span), 2)).astype(F32)
    usable = position < length3
    masked = jnp.where(usable, scores, NEGATIVE)
    best = jnp.max(masked, axis=2, keepdims=True)
    terms = jnp.where(usable, jnp.exp(masked - best), 0.0)
    norm = jnp.sum(terms, axis=2, keepdims=True)
    weighted = jnp.stack([mm(terms[b].astype(BF16), kv[b, 1]) for b in range(requests)])
    lane3 = iota(rows3, 2)
    mine = (lane3 < HD) == (iota(rows3, 1) < group)
    is_best = jnp.logical_and(jnp.logical_not(mine), lane3 % HD < HD // 2)
    is_norm = jnp.logical_and(jnp.logical_not(mine), lane3 % HD >= HD // 2)
    a_buf[row] = jnp.where(mine, weighted, jnp.where(is_best, best, norm))
    copies = spread(a_buf, "row", 2)
    finish(copies)
    bests = [
        jnp.max(jnp.where(is_best, a_buf[k], -3e38), axis=2, keepdims=True) for k in range(n)
    ]
    final_best = own_score
    for value in bests:
        final_best = jnp.maximum(final_best, value)
    own_exp = jnp.exp(own_score - final_best)
    norm_sum = own_exp
    attended = own_exp.astype(BF16).astype(F32) * new_value[:, None, :]
    for k in range(n):
        factor = jnp.exp(bests[k] - final_best)
        message = a_buf[k]
        norm_k = jnp.max(jnp.where(is_norm, message, 0.0), axis=2, keepdims=True)
        norm_sum = norm_sum + norm_k * factor
        attended = attended + message * factor
    q_rows[...] = attended / norm_sum
    att_tiles = []
    for t in range(q_tiles):
        even = q_rows[:, 2 * t, :]
        odd = q_rows[:, 2 * t + 1, :]
        if 2 * t < group:
            att_tiles.append(jnp.where(left, even, pltpu.roll(odd, HD, 1)))
        else:
            att_tiles.append(jnp.where(left, pltpu.roll(even, HD, 1), odd))
    attended2 = jnp.concatenate(att_tiles, axis=1).astype(BF16)

    loads[3].wait()
    o_buf[col] = mm(attended2, wo[...]).astype(BF16)
    finish(spread(o_buf, "col", 3))
    one_float = (x_float + total(o_buf, m)).astype(BF16).astype(F32)

    sq2_buf[row] = squares(one_float)
    sq_copies = spread(sq2_buf, "row", 4)
    mlp_input = (one_float * gains_ref[1:2, :]).astype(BF16)
    loads[4].wait()
    hidden_here = wgu.shape[1] // 2
    block = hidden_here // n
    if block % LANES == 0:
        copies = []
        for k in range(1, n + 1):
            dest = peer("row", k)
            start = pl.multiple_of(dest * block, LANES)
            gate = mm(mlp_input, wgu[:, pl.ds(start, block)])
            up = mm(mlp_input, wgu[:, pl.ds(hidden_here + start, block)])
            joined = jnp.concatenate([gate, up], axis=1).astype(BF16)
            if k < n:
                gu_send[k - 1] = joined
                copies.append(send(gu_send.at[k - 1], gu_buf.at[row], "row", 5, k))
            else:
                gu_buf[row] = joined
        finish(sq_copies)
        mlp_scale = scale_of(total(sq2_buf, n))[:, 0:1]
        finish(copies)
        sums = total(gu_buf, n) * mlp_scale
        gate, up = sums[:, :block], sums[:, block:]
        act_buf[row] = (gate / (1.0 + jnp.exp(-gate)) * up).astype(BF16)
        finish(spread(act_buf, "row", 6))
        loads[5].wait()
        down = mm(act_buf[0], wd[0:block, :])
        for k in range(1, n):
            down = down + mm(act_buf[k], wd[k * block : (k + 1) * block, :])
    else:
        gu_buf[row] = mm(mlp_input, wgu[...]).astype(BF16)
        copies = spread(gu_buf, "row", 5)
        finish(sq_copies)
        mlp_scale = scale_of(total(sq2_buf, n))[:, 0:1]
        finish(copies)
        sums = total(gu_buf, n) * mlp_scale
        gate, up = sums[:, :hidden_here], sums[:, hidden_here:]
        loads[5].wait()
        down = mm((gate / (1.0 + jnp.exp(-gate)) * up).astype(BF16), wd[...])
    d_buf[col] = down.astype(BF16)
    finish(spread(d_buf, "col", 7))
    two_own = (one_float + total(d_buf, m)).astype(BF16)

    two_buf[guide] = two_own
    two_copies = spread(two_buf, "guide", 8)
    own_float = two_own.astype(F32)
    next_input = (own_float * gains_ref[3:4, :]).astype(BF16)
    loads[6].wait()
    np_buf[row, :, 0:width_q] = mm(next_input, wnq[...]).astype(BF16)
    loads[7].wait()
    np_buf[row, :, width_q : width_q + width_kv] = mm(next_input, wnkv[...]).astype(BF16)
    finish(two_copies)
    first = guide == 0

    def my_half(values):
        return jnp.where(first, values[:half_rows], values[half_rows:])

    both = jnp.concatenate(
        [my_half(two_buf[0].astype(F32)), my_half(two_buf[1].astype(F32))], axis=0
    )
    sq3_buf[row] = jnp.where(left, squares(own_float), squares(both))
    sq_copies = spread(sq3_buf, "row", 9)
    np_copies = spread(np_buf, "row", 10)
    head_input = (both * gains_ref[2:3, :]).astype(BF16)

    guidance_row = jnp.zeros((1, requests), F32)
    for k in range(TENANTS):
        guidance_row = guidance_row + jnp.where(tenant_ref[...] == k, guide_ref[k], 0.0)
    here = iota((half_rows, requests), 1) == iota((half_rows, requests), 0) + guide * half_rows
    guidance = jnp.sum(jnp.where(here, guidance_row, 0.0), axis=1, keepdims=True)

    finish(sq_copies)
    scales = scale_of(total(sq3_buf, n))
    own_scale = scales[:, 0:1]
    both_scale = scales[:, LANES - 1 : LANES]
    factor_c = guidance * both_scale[:half_rows]
    factor_u = (1.0 - guidance) * both_scale[half_rows:]

    def guided(rows):
        logits = lax.dot_general(
            head_input, rows, (((1,), (1,)), ((), ())), preferred_element_type=F32
        )
        return factor_c * logits[:half_rows] + factor_u * logits[half_rows:]

    loads[8].wait()
    vocab = wh.shape[0]
    share = vocab // n
    exact = share % SUBLANES == 0
    window = window_of(share)
    half = window // 2
    chunk = 1024 if half % 1024 == 0 else half
    whole = vocab // LANES * LANES
    last_start = (n - 1) * share // LANES * LANES
    copies = []
    if exact:
        part[...] = jnp.zeros(part.shape, F32)
    else:
        part[:, whole : part.shape[1]] = jnp.zeros((half_rows, part.shape[1] - whole), F32)
        if whole < vocab:
            part[:, whole:vocab] = guided(wh[whole:vocab, :])
    for k in range(1, n + 1):
        dest = peer("row", k)
        if exact:
            for piece in range(-(-share // chunk)):
                first_row = piece * chunk
                size = min(chunk, share - first_row)
                at = pl.multiple_of(dest * share + first_row, SUBLANES)
                top = first_row // half * half_rows
                column = first_row % half
                part[top : top + half_rows, column : column + size] = guided(wh[pl.ds(at, size), :])
            stacked = part[...]
        else:
            start = dest * share // LANES * LANES
            is_last = (dest + 1) // n
            for piece in range(window // chunk):
                over = max(0, last_start + (piece + 1) * chunk - whole)
                at = pl.multiple_of(start + piece * chunk - is_last * over, LANES)
                part[:, pl.ds(at, chunk)] = guided(wh[pl.ds(at, chunk), :])
            start = pl.multiple_of(start, LANES)
            upper = pl.multiple_of(start + half, LANES)
            stacked = jnp.concatenate(
                [part[:, pl.ds(start, half)], part[:, pl.ds(upper, half)]], axis=0
            )
        if k < n:
            h_send[k - 1] = stacked.astype(BF16)
            copies.append(send(h_send.at[k - 1], h_buf.at[row], "row", 11, k))
        else:
            h_buf[row] = stacked.astype(BF16)

    finish(np_copies)
    sums = own_scale * total(np_buf, n)
    nq_ref[...] = sums[:, :width_q].astype(BF16)
    nkv_ref[...] = sums[:, width_q:].astype(BF16)

    finish(copies)
    sums = total(h_buf, n)
    if exact:
        out_ref[:, 0:half] = sums[:half_rows]
        out_ref[:, half:share] = sums[half_rows:, 0 : share - half]
    else:
        part[:, 0:half] = sums[:half_rows]
        part[:, half:window] = sums[half_rows:]
        offset = lax.rem(row * share, LANES)
        turn = lax.rem(LANES - offset, LANES)
        lane8 = iota((half_rows, LANES), 1)
        for j in range(-(-share // LANES)):
            here_tile = pltpu.roll(part[:, j * LANES : (j + 1) * LANES], turn, 1)
            next_tile = pltpu.roll(part[:, (j + 1) * LANES : (j + 2) * LANES], turn, 1)
            joined = jnp.where(lane8 < LANES - offset, here_tile, next_tile)
            wide = min(LANES, share - j * LANES)
            out_ref[:, j * LANES : j * LANES + wide] = joined[:, :wide]


def local(
    n,
    m,
    hidden,
    lengths,
    kv_cache,
    attn_gain,
    w_query,
    w_key_value,
    w_out,
    mlp_gain,
    w_gate_up,
    w_down,
    final_gain,
    w_head,
    next_gain,
    w_next_query,
    w_next_kv,
    tenant,
    guide_scale,
):
    x_rows = hidden[0]
    requests, width = x_rows.shape
    gains = jnp.stack([attn_gain, mlp_gain, final_gain, next_gain]).astype(F32)
    w_kv = w_key_value.reshape(width, -1)
    w_gu = w_gate_up.reshape(width, -1)
    w_nkv = w_next_kv.reshape(width, -1)
    cache = kv_cache[0]
    head_rows = w_head.T
    weights = (cache, w_query, w_kv, w_out, w_gu, w_down, head_rows, w_next_query, w_nkv)
    width_q = w_query.shape[1]
    width_kv = w_kv.shape[1]
    heads_here = width_q // HD
    hidden_here = w_down.shape[0]
    block = hidden_here // n
    vocab = head_rows.shape[0]
    share = vocab // n
    window = window_of(share)
    last_start = (n - 1) * share // LANES * LANES
    exact = share % SUBLANES == 0
    part_shape = (requests, window // 2) if exact else (requests // 2, last_start + window)
    scattered = block % LANES == 0
    gu_width = 2 * block if scattered else 2 * hidden_here
    peers = max(n, m) - 1
    vmem = pl.BlockSpec(memory_space=pltpu.VMEM)
    smem = pl.BlockSpec(memory_space=pltpu.SMEM)
    hbm = pl.BlockSpec(memory_space=pl.ANY)
    scratch = [pltpu.VMEM(a.shape, a.dtype) for a in weights] + [
        pltpu.VMEM((n, requests, width_q + width_kv), BF16),
        pltpu.VMEM((n, requests, LANES), F32),
        pltpu.VMEM((requests, heads_here, LANES), F32),
        pltpu.VMEM((n, requests, heads_here, LANES), F32),
        pltpu.VMEM((m, requests, width), BF16),
        pltpu.VMEM((n, requests, LANES), F32),
        pltpu.VMEM((n - 1 if scattered else 1, requests, gu_width), BF16),
        pltpu.VMEM((n, requests, gu_width), BF16),
        pltpu.VMEM((n, requests, block), BF16),
        pltpu.VMEM((m, requests, width), BF16),
        pltpu.VMEM((2, requests, width), BF16),
        pltpu.VMEM((n, requests, LANES), F32),
        pltpu.VMEM((n, requests, width_q + width_kv), BF16),
        pltpu.VMEM(part_shape, F32),
        pltpu.VMEM((n - 1, requests, window // 2), BF16),
        pltpu.VMEM((n, requests, window // 2), BF16),
        pltpu.SemaphoreType.DMA((9,)),
        pltpu.SemaphoreType.DMA((12, peers)),
        pltpu.SemaphoreType.DMA((12, peers)),
    ]
    guided, next_query, next_pairs = pl.pallas_call(
        functools.partial(layer_kernel, n, m),
        out_shape=(
            jax.ShapeDtypeStruct((requests // 2, share), F32),
            jax.ShapeDtypeStruct((requests, width_q), BF16),
            jax.ShapeDtypeStruct((requests, width_kv), BF16),
        ),
        in_specs=[vmem, vmem, vmem, smem, vmem] + [hbm] * 9,
        out_specs=(vmem, vmem, vmem),
        scratch_shapes=scratch,
        compiler_params=pltpu.CompilerParams(
            collective_id=0, has_side_effects=True, vmem_limit_bytes=60 * 1024 * 1024
        ),
        name="decode_layer",
    )(x_rows, lengths, tenant.reshape(1, -1), guide_scale, gains, *weights)
    return (guided, next_query[None], next_pairs.reshape(1, requests, 2, -1))


def solution(mesh):
    placed = (
        P("guide", None, "row"),
        P("guide", None),
        P("guide", None, None, "row", "col"),
        P("row"),
        P("row", "col"),
        P("row", None, "col"),
        P("col", "row"),
        P("row"),
        P("row", None, "col"),
        P("col", "row"),
        P("row"),
        P("row", "col"),
        P("row"),
        P("row", "col"),
        P("row", None, "col"),
        P(),
        P(),
    )
    return jax.shard_map(
        functools.partial(local, mesh.shape["row"], mesh.shape["col"]),
        mesh=mesh,
        in_specs=placed,
        out_specs=(
            P("guide", ("col", "row")),
            P("guide", None, "col"),
            P("guide", None, None, "col"),
        ),
        check_vma=False,
    )
```

time: 473 us -> 70.9 us (0.15)
  waiting for transfers between devices: 304 us -> 0 us
  blocking collectives: 92 us -> 0 us
  Pallas kernels: 0 us -> 53.8 us
  matrix products: 31 us -> 0 us
  between operations: 14.3 us -> 0.64 us
  local copies, waits for them, and re-layouts: 22.9 us -> 15.4 us
  other arithmetic: 5.49 us -> 0.61 us
    unnamed x3 -> x0, waiting for transfers between devices: 265 us -> none
    psum x5 -> x0, blocking collectives: 60.1 us -> none  [the longest x1 13 us: local(): lax.psum((query_part, pair_part, squares(x_float)), 'row')]
    pallas_call x0 -> x1, Pallas kernels: none -> 53.8 us  [local(): pl.pallas_call(functools.partial(layer_kernel, n, m), out_shape=(jax.Shap...]
    psum x1 -> x0, waiting for transfers between devices: 39.5 us -> none  [local(): gate_up, second_squares = lax.psum((gate_part, squares(one_float)), 'row')]
    all_gather x3 -> x0, blocking collectives: 31.9 us -> none  [joined(): everything = jax.tree.map(lambda part: lax.all_gather(part, axis), x)]
    unnamed x1 -> x0, matrix products: 20.5 us -> none
    dot_general x10 -> x0, matrix products: 10.4 us -> none  [the longest x1 4.08 us: local(): jnp.dot(mlp_input, w_gate_up.reshape(local_width, -1), preferred_element_...]
    dot_general x2 -> x0, local copies, waits for them, and re-layouts: 6.57 us -> none  [the longest x1 6.47 us: local(): jnp.dot(mlp_input, w_gate_up.reshape(local_width, -1), preferred_element_...]
  transfers between devices with their start and end apart: 3 -> 0, of which waited for: 2 -> 0; matrix products, arithmetic and copies ran while one was open for 0% -> 0% of each run, Pallas kernels for 0% -> 0%
where the time goes in v1:
time: 70.9 us; the launch traced here: 70.4 us
  Pallas kernels  53.8 us (76%)
  local copies, waits for them, and re-layouts  15.4 us (22%)
    pallas_call x1, Pallas kernels, local(): pl.pallas_call(functools.partial(layer_kernel, n, m), out_shape=(jax.Shap...  53.8 us
    unnamed x3, local copies, waits for them, and re-layouts  9.5 us
    another operation x4, local copies, waits for them, and re-layouts, local(): gains = jnp.stack([attn_gain, mlp_gain, final_gain, next_gain]).astype(F32)  2.73 us
    reshape x1, local copies, waits for them, and re-layouts, local(): w_nkv = w_next_kv.reshape(width, -1)  1.9 us

profile of v1, /device:TPU:9, one launch (start us, length us, event | category | flops | bytes accessed | tf_op | source)
XLA Modules:
  0.0 70.4 jit_solution(11137057710211606896)
XLA Ops:
  0.6 0.7 stack.15
  1.3 0.7 stack.16
  2.0 0.7 stack.17
  2.7 0.7 stack.18
  3.4 0.6 maximum_convert_fusion.gains_ref
  4.0 1.9 %copy_bitcast_fusion = (bf16[512,256]{1,0:T(8,128)(2,1)}, bf16[512,256]{1,0:T(8,128)(2,1)}) fusion(bf16[64,8,2,128]{3,2,1,0:T(2,128)(2,1)} %bitcast.17, bf16[64,8,2,128]{3,2,1,0:T(2,128)(2,1)} %bitcast.18), kind=kLoop, calls=%fused_computation | loop fusion | bytes 1048576 | tf_op jit(solution)/shard_map/reshape | solution.py:438
  5.9 6.5 %copy.21 = bf16[64,8,2,2048]{3,1,2,0:T(8,128)(2,1)} copy(bf16[64,8,2,2048]{3,2,1,0:T(2,128)(2,1)} %bitcast.15) | data formatting | bytes 8388608
  12.4 53.8 %decode_layer.1 = (f32[8,8016]{1,0:T(8,128)}, bf16[16,512]{1,0:T(8,128)(2,1)}, bf16[16,256]{1,0:T(8,128)(2,1)}) custom-call(bf16[16,512]{1,0:T(8,128)(2,1)} %bitcast.19, s32[1,16]{1,0:T(1,128)} %len_ref.1, s32[1,16]{1,0:T(1,128)} %bitcast.21, f32[4]{0:T(128)} %guide_ref.1, f32[4,512]{1,0:T(4,128)} %maximum_convert_fusion.gains_ref, ...), custom_call_target="tpu_custom_call" | custom-call | tf_op jit(solution)/shard_map/decode_layer/pallas_call | solution.py:480
  66.2 1.3 %reshape.25 = bf16[1,16,2,128]{3,2,1,0:T(2,128)(2,1)} reshape(bf16[16,256]{1,0:T(8,128)(2,1)} %get-tuple-element.8) | data formatting | bytes 16384 | tf_op jit(solution)/shard_map/reshape | solution.py:495
  67.5 1.7 %copy.27 = f32[8,8016]{1,0:T(8,128)} copy(f32[8,8016]{1,0:T(8,128)} %get-tuple-element.14) | data formatting | bytes 513024
  69.1 1.3 %copy.28 = bf16[1,16,512]{2,1,0:T(8,128)(2,1)} copy(bf16[1,16,512]{2,1,0:T(8,128)(2,1)} %bitcast.20) | data formatting | bytes 32768

commit v2 on v1

--- a/solution.py
+++ b/solution.py
@@ -43,7 +43,10 @@
     len_ref,
     tenant_ref,
     guide_ref,
-    gains_ref,
+    attn_gain_ref,
+    mlp_gain_ref,
+    final_gain_ref,
+    next_gain_ref,
     kv_hbm,
     wq_hbm,
     wkv_hbm,
@@ -65,9 +68,11 @@
     wh,
     wnq,
     wnkv,
+    weaver,
     q_buf,
     sq_buf,
     q_rows,
+    stat_buf,
     a_buf,
     o_buf,
     sq2_buf,
@@ -78,12 +83,14 @@
     two_buf,
     sq3_buf,
     np_buf,
+    first_part,
     part,
     h_send,
     h_buf,
     local_sem,
     send_sem,
     recv_sem,
+    sq_sem,
 ):
     row = lax.axis_index("row")
     col = lax.axis_index("col")
@@ -99,17 +106,34 @@
         (wd_hbm, wd),
         (wnq_hbm, wnq),
         (wnkv_hbm, wnkv),
-        (wh_hbm, wh),
     ]
     loads = [pltpu.make_async_copy(a, b, local_sem.at[i]) for i, (a, b) in enumerate(pairs)]
     for load in loads:
         load.start()
+    share = wh.shape[0] // n
+    exact = share % SUBLANES == 0
+    if exact:
+        head_loads = []
+        for k in range(1, n + 1):
+            at = pl.ds(pl.multiple_of(lax.rem(row + k, n) * share, SUBLANES), share)
+            head_loads.append(
+                pltpu.make_async_copy(wh_hbm.at[at, :], wh.at[at, :], local_sem.at[7 + k])
+            )
+    else:
+        head_loads = [pltpu.make_async_copy(wh_hbm, wh, local_sem.at[8])]
+    early = (len(head_loads) + 1) // 2
+
+    pending = []
 
     def peer(axis, k):
         me, size = place[axis]
         return lax.rem(me + k, size)
 
+    other = 1 - guide
     barrier = pltpu.get_barrier_semaphore()
+    for k in range(1, n):
+        target = {"row": peer("row", k), "guide": other}
+        pl.semaphore_signal(barrier, inc=1, device_id=target, device_id_type=MESH)
     for axis in ("row", "col", "guide"):
         for k in range(1, place[axis][1]):
             pl.semaphore_signal(barrier, inc=1, device_id={axis: peer(axis, k)}, device_id_type=MESH)
@@ -132,7 +156,8 @@
 
     def finish(copies):
         for copy in copies:
-            copy.wait()
+            copy.wait_recv()
+            pending.append(copy)
 
     def total(buf, size):
         result = buf[0].astype(F32)
@@ -147,18 +172,33 @@
         return lax.rsqrt(sums / D + EPSILON)
 
     requests = x_ref.shape[0]
+    depth = wgu.shape[0]
+    width_q = wq.shape[1]
+    key_width = wkv.shape[2]
+    width_kv = 2 * key_width
+    weaver[...] = (iota((depth, 2 * depth), 1) == 2 * iota((depth, 2 * depth), 0)).astype(BF16)
+
+    def weave(values):
+        even = mm(values, weaver[...])
+        return jnp.concatenate([even, pltpu.roll(even, 1, 1)], axis=0).astype(BF16)
+
+    def pairs_to(buf, values, weights):
+        both_parts = mm(weave(values), weights[...].reshape(2 * depth, weights.shape[2]))
+        buf[row, :, width_q : width_q + key_width] = both_parts[:requests].astype(BF16)
+        buf[row, :, width_q + key_width : width_q + width_kv] = both_parts[requests:].astype(BF16)
+
     half_rows = requests // 2
     x_float = x_ref[...].astype(F32)
-    normed = (x_float * gains_ref[0:1, :]).astype(BF16)
+    normed = (x_float * attn_gain_ref[...].astype(F32)[None, :]).astype(BF16)
     sq_buf[row] = squares(x_float)
     loads[0].wait()
-    width_q = wq.shape[1]
-    width_kv = wkv.shape[1]
     q_buf[row, :, 0:width_q] = mm(normed, wq[...]).astype(BF16)
     loads[1].wait()
-    q_buf[row, :, width_q : width_q + width_kv] = mm(normed, wkv[...]).astype(BF16)
-    pl.semaphore_wait(barrier, n - 1 + m - 1 + 1)
+    pairs_to(q_buf, normed, wkv)
+    pl.semaphore_wait(barrier, 2 * (n - 1) + m - 1 + 1)
     copies = spread(sq_buf, "row", 0) + spread(q_buf, "row", 1)
+    for load in head_loads[:early]:
+        load.start()
 
     lane = iota((requests, LANES), 1)
     lengths_row = len_ref[...].astype(F32)
@@ -218,36 +258,46 @@
     norm = jnp.sum(terms, axis=2, keepdims=True)
     weighted = jnp.stack([mm(terms[b].astype(BF16), kv[b, 1]) for b in range(requests)])
     lane3 = iota(rows3, 2)
-    mine = (lane3 < HD) == (iota(rows3, 1) < group)
-    is_best = jnp.logical_and(jnp.logical_not(mine), lane3 % HD < HD // 2)
-    is_norm = jnp.logical_and(jnp.logical_not(mine), lane3 % HD >= HD // 2)
-    a_buf[row] = jnp.where(mine, weighted, jnp.where(is_best, best, norm))
-    copies = spread(a_buf, "row", 2)
-    finish(copies)
-    bests = [
-        jnp.max(jnp.where(is_best, a_buf[k], -3e38), axis=2, keepdims=True) for k in range(n)
-    ]
-    final_best = own_score
-    for value in bests:
-        final_best = jnp.maximum(final_best, value)
-    own_exp = jnp.exp(own_score - final_best)
-    norm_sum = own_exp
-    attended = own_exp.astype(BF16).astype(F32) * new_value[:, None, :]
-    for k in range(n):
-        factor = jnp.exp(bests[k] - final_best)
-        message = a_buf[k]
-        norm_k = jnp.max(jnp.where(is_norm, message, 0.0), axis=2, keepdims=True)
-        norm_sum = norm_sum + norm_k * factor
-        attended = attended + message * factor
-    q_rows[...] = attended / norm_sum
-    att_tiles = []
+    q_rows[...] = weighted
+
+    def to_lanes(column):
+        return jnp.sum(jnp.where(lane3 == iota(rows3, 1), column, 0.0), axis=1)
+
+    def by_head(table, t):
+        return jnp.where(left, table[:, 2 * t : 2 * t + 1], table[:, 2 * t + 1 : 2 * t + 2])
+
+    stat_buf[row] = jnp.where(left, to_lanes(best), pltpu.roll(to_lanes(norm), HD, 1))
     for t in range(q_tiles):
         even = q_rows[:, 2 * t, :]
         odd = q_rows[:, 2 * t + 1, :]
         if 2 * t < group:
-            att_tiles.append(jnp.where(left, even, pltpu.roll(odd, HD, 1)))
+            tile = jnp.where(left, even, pltpu.roll(odd, HD, 1))
         else:
-            att_tiles.append(jnp.where(left, pltpu.roll(even, HD, 1), odd))
+            tile = jnp.where(left, pltpu.roll(even, HD, 1), odd)
+        a_buf[row, :, t * LANES : (t + 1) * LANES] = tile.astype(BF16)
+    copies = spread(stat_buf, "row", 12) + spread(a_buf, "row", 2)
+    for load in head_loads[early:]:
+        load.start()
+    own_lanes = to_lanes(own_score)
+    turned_value = pltpu.roll(new_value, HD, 1)
+    value_of = (jnp.where(left, new_value, turned_value), jnp.where(left, turned_value, new_value))
+    finish(copies)
+    bests = [stat_buf[k] for k in range(n)]
+    final_best = own_lanes
+    for value in bests:
+        final_best = jnp.maximum(final_best, value)
+    own_exp = jnp.exp(own_lanes - final_best)
+    factors = [jnp.exp(value - final_best) for value in bests]
+    norm_sum = own_exp
+    for k in range(n):
+        norm_sum = norm_sum + pltpu.roll(bests[k], HD, 1) * factors[k]
+    own_factor = own_exp.astype(BF16).astype(F32)
+    att_tiles = []
+    for t in range(q_tiles):
+        tile = by_head(own_factor, t) * value_of[2 * t // group]
+        for k in range(n):
+            tile = tile + by_head(factors[k], t) * a_buf[k, :, t * LANES : (t + 1) * LANES].astype(F32)
+        att_tiles.append(tile / by_head(norm_sum, t))
     attended2 = jnp.concatenate(att_tiles, axis=1).astype(BF16)
 
     loads[3].wait()
@@ -257,18 +307,19 @@
 
     sq2_buf[row] = squares(one_float)
     sq_copies = spread(sq2_buf, "row", 4)
-    mlp_input = (one_float * gains_ref[1:2, :]).astype(BF16)
+    mlp_input = (one_float * mlp_gain_ref[...].astype(F32)[None, :]).astype(BF16)
     loads[4].wait()
-    hidden_here = wgu.shape[1] // 2
+    hidden_here = wgu.shape[2]
     block = hidden_here // n
+    woven = weave(mlp_input)
     if block % LANES == 0:
         copies = []
         for k in range(1, n + 1):
             dest = peer("row", k)
             start = pl.multiple_of(dest * block, LANES)
-            gate = mm(mlp_input, wgu[:, pl.ds(start, block)])
-            up = mm(mlp_input, wgu[:, pl.ds(hidden_here + start, block)])
-            joined = jnp.concatenate([gate, up], axis=1).astype(BF16)
+            rows = wgu[:, :, pl.ds(start, block)].reshape(2 * wgu.shape[0], block)
+            both_parts = mm(woven, rows)
+            joined = jnp.concatenate([both_parts[:requests], both_parts[requests:]], axis=1).astype(BF16)
             if k < n:
                 gu_send[k - 1] = joined
                 copies.append(send(gu_send.at[k - 1], gu_buf.at[row], "row", 5, k))
@@ -286,7 +337,9 @@
         for k in range(1, n):
             down = down + mm(act_buf[k], wd[k * block : (k + 1) * block, :])
     else:
-        gu_buf[row] = mm(mlp_input, wgu[...]).astype(BF16)
+        both_parts = mm(woven, wgu[...].reshape(2 * wgu.shape[0], hidden_here))
+        gu_buf[row, :, 0:hidden_here] = both_parts[:requests].astype(BF16)
+        gu_buf[row, :, hidden_here : 2 * hidden_here] = both_parts[requests:].astype(BF16)
         copies = spread(gu_buf, "row", 5)
         finish(sq_copies)
         mlp_scale = scale_of(total(sq2_buf, n))[:, 0:1]
@@ -302,11 +355,28 @@
     two_buf[guide] = two_own
     two_copies = spread(two_buf, "guide", 8)
     own_float = two_own.astype(F32)
-    next_input = (own_float * gains_ref[3:4, :]).astype(BF16)
+    sq3_buf[guide, row] = squares(own_float)
+    sq_copies = []
+    for k in range(n):
+        targets = [{"row": peer("row", k), "guide": other}]
+        if k:
+            targets.append({"row": peer("row", k)})
+        for number, target in zip((0, 1), targets):
+            copy = pltpu.make_async_remote_copy(
+                src_ref=sq3_buf.at[guide, row],
+                dst_ref=sq3_buf.at[guide, row],
+                send_sem=sq_sem.at[0, number, k],
+                recv_sem=sq_sem.at[1, number, k],
+                device_id=target,
+                device_id_type=MESH,
+            )
+            copy.start()
+            sq_copies.append(copy)
+    next_input = (own_float * next_gain_ref[...].astype(F32)[None, :]).astype(BF16)
     loads[6].wait()
     np_buf[row, :, 0:width_q] = mm(next_input, wnq[...]).astype(BF16)
     loads[7].wait()
-    np_buf[row, :, width_q : width_q + width_kv] = mm(next_input, wnkv[...]).astype(BF16)
+    pairs_to(np_buf, next_input, wnkv)
     finish(two_copies)
     first = guide == 0
 
@@ -316,10 +386,8 @@
     both = jnp.concatenate(
         [my_half(two_buf[0].astype(F32)), my_half(two_buf[1].astype(F32))], axis=0
     )
-    sq3_buf[row] = jnp.where(left, squares(own_float), squares(both))
-    sq_copies = spread(sq3_buf, "row", 9)
     np_copies = spread(np_buf, "row", 10)
-    head_input = (both * gains_ref[2:3, :]).astype(BF16)
+    head_input = (both * final_gain_ref[...].astype(F32)[None, :]).astype(BF16)
 
     guidance_row = jnp.zeros((1, requests), F32)
     for k in range(TENANTS):
@@ -327,45 +395,56 @@
     here = iota((half_rows, requests), 1) == iota((half_rows, requests), 0) + guide * half_rows
     guidance = jnp.sum(jnp.where(here, guidance_row, 0.0), axis=1, keepdims=True)
 
-    finish(sq_copies)
-    scales = scale_of(total(sq3_buf, n))
-    own_scale = scales[:, 0:1]
-    both_scale = scales[:, LANES - 1 : LANES]
-    factor_c = guidance * both_scale[:half_rows]
-    factor_u = (1.0 - guidance) * both_scale[half_rows:]
-
-    def guided(rows):
-        logits = lax.dot_general(
+    def raw(rows):
+        return lax.dot_general(
             head_input, rows, (((1,), (1,)), ((), ())), preferred_element_type=F32
         )
-        return factor_c * logits[:half_rows] + factor_u * logits[half_rows:]
-
-    loads[8].wait()
+
     vocab = wh.shape[0]
-    share = vocab // n
-    exact = share % SUBLANES == 0
     window = window_of(share)
     half = window // 2
     chunk = 1024 if half % 1024 == 0 else half
     whole = vocab // LANES * LANES
     last_start = (n - 1) * share // LANES * LANES
+    pieces = [(at, min(chunk, share - at)) for at in range(0, share, chunk)]
     copies = []
+    head_loads[0].wait()
     if exact:
         part[...] = jnp.zeros(part.shape, F32)
-    else:
+        for at, size in pieces:
+            start = pl.multiple_of(peer("row", 1) * share + at, SUBLANES)
+            first_part[:, at : at + size] = raw(wh[pl.ds(start, size), :])
+
+    finish(sq_copies)
+    sums = [total(sq3_buf.at[side], n) for side in range(2)]
+    own_scale = scale_of(jnp.where(first, sums[0], sums[1]))[:, 0:1]
+    factor_c = guidance * scale_of(my_half(sums[0]))[:, 0:1]
+    factor_u = (1.0 - guidance) * scale_of(my_half(sums[1]))[:, 0:1]
+
+    def blend(logits):
+        return factor_c * logits[:half_rows] + factor_u * logits[half_rows:]
+
+    def guided(rows):
+        return blend(raw(rows))
+
+    if not exact:
         part[:, whole : part.shape[1]] = jnp.zeros((half_rows, part.shape[1] - whole), F32)
         if whole < vocab:
             part[:, whole:vocab] = guided(wh[whole:vocab, :])
     for k in range(1, n + 1):
         dest = peer("row", k)
         if exact:
-            for piece in range(-(-share // chunk)):
-                first_row = piece * chunk
-                size = min(chunk, share - first_row)
+            if k > 1:
+                head_loads[k - 1].wait()
+            for first_row, size in pieces:
                 at = pl.multiple_of(dest * share + first_row, SUBLANES)
                 top = first_row // half * half_rows
                 column = first_row % half
-                part[top : top + half_rows, column : column + size] = guided(wh[pl.ds(at, size), :])
+                if k == 1:
+                    value = blend(first_part[:, first_row : first_row + size])
+                else:
+                    value = guided(wh[pl.ds(at, size), :])
+                part[top : top + half_rows, column : column + size] = value
             stacked = part[...]
         else:
             start = dest * share // LANES * LANES
@@ -407,6 +486,8 @@
             joined = jnp.where(lane8 < LANES - offset, here_tile, next_tile)
             wide = min(LANES, share - j * LANES)
             out_ref[:, j * LANES : j * LANES + wide] = joined[:, :wide]
+    for copy in pending:
+        copy.wait_send()
 
 
 def local(
@@ -432,15 +513,11 @@
 ):
     x_rows = hidden[0]
     requests, width = x_rows.shape
-    gains = jnp.stack([attn_gain, mlp_gain, final_gain, next_gain]).astype(F32)
-    w_kv = w_key_value.reshape(width, -1)
-    w_gu = w_gate_up.reshape(width, -1)
-    w_nkv = w_next_kv.reshape(width, -1)
     cache = kv_cache[0]
     head_rows = w_head.T
-    weights = (cache, w_query, w_kv, w_out, w_gu, w_down, head_rows, w_next_query, w_nkv)
+    weights = (cache, w_query, w_key_value, w_out, w_gate_up, w_down, head_rows, w_next_query, w_next_kv)
     width_q = w_query.shape[1]
-    width_kv = w_kv.shape[1]
+    width_kv = 2 * w_key_value.shape[2]
     heads_here = width_q // HD
     hidden_here = w_down.shape[0]
     block = hidden_here // n
@@ -450,6 +527,7 @@
     last_start = (n - 1) * share // LANES * LANES
     exact = share % SUBLANES == 0
     part_shape = (requests, window // 2) if exact else (requests // 2, last_start + window)
+    first_shape = (requests, window) if exact else (requests, LANES)
     scattered = block % LANES == 0
     gu_width = 2 * block if scattered else 2 * hidden_here
     peers = max(n, m) - 1
@@ -457,10 +535,12 @@
     smem = pl.BlockSpec(memory_space=pltpu.SMEM)
     hbm = pl.BlockSpec(memory_space=pl.ANY)
     scratch = [pltpu.VMEM(a.shape, a.dtype) for a in weights] + [
+        pltpu.VMEM((width, 2 * width), BF16),
         pltpu.VMEM((n, requests, width_q + width_kv), BF16),
         pltpu.VMEM((n, requests, LANES), F32),
         pltpu.VMEM((requests, heads_here, LANES), F32),
-        pltpu.VMEM((n, requests, heads_here, LANES), F32),
+        pltpu.VMEM((n, requests, LANES), F32),
+        pltpu.VMEM((n, requests, width_q), BF16),
         pltpu.VMEM((m, requests, width), BF16),
         pltpu.VMEM((n, requests, LANES), F32),
         pltpu.VMEM((n - 1 if scattered else 1, requests, gu_width), BF16),
@@ -468,14 +548,16 @@
         pltpu.VMEM((n, requests, block), BF16),
         pltpu.VMEM((m, requests, width), BF16),
         pltpu.VMEM((2, requests, width), BF16),
-        pltpu.VMEM((n, requests, LANES), F32),
+        pltpu.VMEM((2, n, requests, LANES), F32),
         pltpu.VMEM((n, requests, width_q + width_kv), BF16),
+        pltpu.VMEM(first_shape, F32),
         pltpu.VMEM(part_shape, F32),
         pltpu.VMEM((n - 1, requests, window // 2), BF16),
         pltpu.VMEM((n, requests, window // 2), BF16),
-        pltpu.SemaphoreType.DMA((9,)),
-        pltpu.SemaphoreType.DMA((12, peers)),
-        pltpu.SemaphoreType.DMA((12, peers)),
+        pltpu.SemaphoreType.DMA((8 + n,)),
+        pltpu.SemaphoreType.DMA((14, peers)),
+        pltpu.SemaphoreType.DMA((14, peers)),
+        pltpu.SemaphoreType.DMA((2, 2, n)),
     ]
     guided, next_query, next_pairs = pl.pallas_call(
         functools.partial(layer_kernel, n, m),
@@ -484,14 +566,14 @@
             jax.ShapeDtypeStruct((requests, width_q), BF16),
             jax.ShapeDtypeStruct((requests, width_kv), BF16),
         ),
-        in_specs=[vmem, vmem, vmem, smem, vmem] + [hbm] * 9,
+        in_specs=[vmem, vmem, vmem, smem] + [vmem] * 4 + [hbm] * 9,
         out_specs=(vmem, vmem, vmem),
         scratch_shapes=scratch,
         compiler_params=pltpu.CompilerParams(
             collective_id=0, has_side_effects=True, vmem_limit_bytes=60 * 1024 * 1024
         ),
         name="decode_layer",
-    )(x_rows, lengths, tenant.reshape(1, -1), guide_scale, gains, *weights)
+    )(x_rows, lengths, tenant.reshape(1, -1), guide_scale, attn_gain, mlp_gain, final_gain, next_gain, *weights)
     return (guided, next_query[None], next_pairs.reshape(1, requests, 2, -1))
 
 

time: 70.9 us -> 55.3 us (0.78)
  local copies, waits for them, and re-layouts: 15.4 us -> 4.29 us
  Pallas kernels: 53.8 us -> 50 us
    unnamed x3 -> x2, local copies, waits for them, and re-layouts: 9.5 us -> 2.98 us
    pallas_call x1, Pallas kernels: 53.8 us -> 50 us  [local(): pl.pallas_call(functools.partial(layer_kernel, n, m), out_shape=(jax.Shap...]
    another operation x4 -> x0, local copies, waits for them, and re-layouts: 2.73 us -> none  [local(): gains = jnp.stack([attn_gain, mlp_gain, final_gain, next_gain]).astype(F32)]
    reshape x1 -> x0, local copies, waits for them, and re-layouts: 1.9 us -> none  [local(): w_nkv = w_next_kv.reshape(width, -1)]
where the time goes in v2:
time: 55.3 us; the launch traced here: 54.9 us
  Pallas kernels  50 us (90%)
  local copies, waits for them, and re-layouts  4.29 us (8%)
  between operations  0.65 us (1%)
    pallas_call x1, Pallas kernels, local(): pl.pallas_call(functools.partial(layer_kernel, n, m), out_shape=(jax.Shap...  50 us
    unnamed x2, local copies, waits for them, and re-layouts  2.98 us
    reshape x1, local copies, waits for them, and re-layouts, local(): return (guided, next_query[None], next_pairs.reshape(1, requests, 2, -1))  1.3 us

profile of v2, /device:TPU:9, one launch (start us, length us, event | category | flops | bytes accessed | tf_op | source)
XLA Modules:
  0.0 54.9 jit_solution(14366992286958397933)
XLA Ops:
  0.6 50.0 %decode_layer.1 = (f32[8,8016]{1,0:T(8,128)}, bf16[16,512]{1,0:T(8,128)(2,1)}, bf16[16,256]{1,0:T(8,128)(2,1)}) custom-call(bf16[16,512]{1,0:T(8,128)(2,1)} %bitcast.7, s32[1,16]{1,0:T(1,128)} %len_ref.1, s32[1,16]{1,0:T(1,128)} %bitcast.9, f32[4]{0:T(128)} %guide_ref.1, bf16[512]{0:T(512)(128)(2,1)} %attn_gain_ref.1, bf16[512]{0:T(512)(128)(2,1)} %mlp_gain_ref.1, ...), custom_call_target="tpu_custom_call" | custom-call | tf_op jit(solution)/shard_map/decode_layer/pallas_call | solution.py:562
  50.7 1.3 %reshape.13 = bf16[1,16,2,128]{3,2,1,0:T(2,128)(2,1)} reshape(bf16[16,256]{1,0:T(8,128)(2,1)} %get-tuple-element.8) | data formatting | bytes 16384 | tf_op jit(solution)/shard_map/reshape | solution.py:577
  52.0 1.7 %copy.22 = f32[8,8016]{1,0:T(8,128)} copy(f32[8,8016]{1,0:T(8,128)} %get-tuple-element.12) | data formatting | bytes 513024
  53.6 1.3 %copy.23 = bf16[1,16,512]{2,1,0:T(8,128)(2,1)} copy(bf16[1,16,512]{2,1,0:T(8,128)(2,1)} %bitcast.8) | data formatting | bytes 32768

commit v3 on v2

--- a/solution.py
+++ b/solution.py
@@ -57,8 +57,7 @@
     wnq_hbm,
     wnkv_hbm,
     out_ref,
-    nq_ref,
-    nkv_ref,
+    next_ref,
     kv,
     wq,
     wkv,
@@ -69,6 +68,7 @@
     wnq,
     wnkv,
     weaver,
+    flat,
     q_buf,
     sq_buf,
     q_rows,
@@ -80,7 +80,7 @@
     gu_buf,
     act_buf,
     d_buf,
-    two_buf,
+    one_buf,
     sq3_buf,
     np_buf,
     first_part,
@@ -90,7 +90,7 @@
     local_sem,
     send_sem,
     recv_sem,
-    sq_sem,
+    d_sem,
 ):
     row = lax.axis_index("row")
     col = lax.axis_index("col")
@@ -131,8 +131,8 @@
 
     other = 1 - guide
     barrier = pltpu.get_barrier_semaphore()
-    for k in range(1, n):
-        target = {"row": peer("row", k), "guide": other}
+    for k in range(1, m):
+        target = {"col": peer("col", k), "guide": other}
         pl.semaphore_signal(barrier, inc=1, device_id=target, device_id_type=MESH)
     for axis in ("row", "col", "guide"):
         for k in range(1, place[axis][1]):
@@ -182,6 +182,11 @@
         even = mm(values, weaver[...])
         return jnp.concatenate([even, pltpu.roll(even, 1, 1)], axis=0).astype(BF16)
 
+    def flatten(low_row, high_row):
+        flat[2 * low_row : 2 * high_row, :] = wgu[low_row:high_row].reshape(
+            2 * (high_row - low_row), wgu.shape[2]
+        )
+
     def pairs_to(buf, values, weights):
         both_parts = mm(weave(values), weights[...].reshape(2 * depth, weights.shape[2]))
         buf[row, :, width_q : width_q + key_width] = both_parts[:requests].astype(BF16)
@@ -195,7 +200,7 @@
     q_buf[row, :, 0:width_q] = mm(normed, wq[...]).astype(BF16)
     loads[1].wait()
     pairs_to(q_buf, normed, wkv)
-    pl.semaphore_wait(barrier, 2 * (n - 1) + m - 1 + 1)
+    pl.semaphore_wait(barrier, n - 1 + 2 * (m - 1) + 1)
     copies = spread(sq_buf, "row", 0) + spread(q_buf, "row", 1)
     for load in head_loads[:early]:
         load.start()
@@ -279,6 +284,9 @@
     for load in head_loads[early:]:
         load.start()
     own_lanes = to_lanes(own_score)
+    loads[4].wait()
+    hidden_here = wgu.shape[2]
+    flatten(0, depth // 2)
     turned_value = pltpu.roll(new_value, HD, 1)
     value_of = (jnp.where(left, new_value, turned_value), jnp.where(left, turned_value, new_value))
     finish(copies)
@@ -302,14 +310,17 @@
 
     loads[3].wait()
     o_buf[col] = mm(attended2, wo[...]).astype(BF16)
-    finish(spread(o_buf, "col", 3))
+    copies = spread(o_buf, "col", 3)
+    flatten(depth // 2, depth)
+    finish(copies)
     one_float = (x_float + total(o_buf, m)).astype(BF16).astype(F32)
+
+    one_buf[guide] = one_float.astype(BF16)
+    one_copies = spread(one_buf, "guide", 8)
 
     sq2_buf[row] = squares(one_float)
     sq_copies = spread(sq2_buf, "row", 4)
     mlp_input = (one_float * mlp_gain_ref[...].astype(F32)[None, :]).astype(BF16)
-    loads[4].wait()
-    hidden_here = wgu.shape[2]
     block = hidden_here // n
     woven = weave(mlp_input)
     if block % LANES == 0:
@@ -317,8 +328,7 @@
         for k in range(1, n + 1):
             dest = peer("row", k)
             start = pl.multiple_of(dest * block, LANES)
-            rows = wgu[:, :, pl.ds(start, block)].reshape(2 * wgu.shape[0], block)
-            both_parts = mm(woven, rows)
+            both_parts = mm(woven, flat[:, pl.ds(start, block)])
             joined = jnp.concatenate([both_parts[:requests], both_parts[requests:]], axis=1).astype(BF16)
             if k < n:
                 gu_send[k - 1] = joined
@@ -331,13 +341,16 @@
         sums = total(gu_buf, n) * mlp_scale
         gate, up = sums[:, :block], sums[:, block:]
         act_buf[row] = (gate / (1.0 + jnp.exp(-gate)) * up).astype(BF16)
-        finish(spread(act_buf, "row", 6))
+        copies = spread(act_buf, "row", 6)
         loads[5].wait()
-        down = mm(act_buf[0], wd[0:block, :])
+        down = mm(act_buf[row], wd[pl.ds(pl.multiple_of(row * block, LANES), block), :])
         for k in range(1, n):
-            down = down + mm(act_buf[k], wd[k * block : (k + 1) * block, :])
+            finish(copies[k - 1 : k])
+            source = lax.rem(row - k + n, n)
+            start = pl.multiple_of(source * block, LANES)
+            down = down + mm(act_buf[source], wd[pl.ds(start, block), :])
     else:
-        both_parts = mm(woven, wgu[...].reshape(2 * wgu.shape[0], hidden_here))
+        both_parts = mm(woven, flat[...])
         gu_buf[row, :, 0:hidden_here] = both_parts[:requests].astype(BF16)
         gu_buf[row, :, hidden_here : 2 * hidden_here] = both_parts[requests:].astype(BF16)
         copies = spread(gu_buf, "row", 5)
@@ -348,43 +361,45 @@
         gate, up = sums[:, :hidden_here], sums[:, hidden_here:]
         loads[5].wait()
         down = mm((gate / (1.0 + jnp.exp(-gate)) * up).astype(BF16), wd[...])
-    d_buf[col] = down.astype(BF16)
-    finish(spread(d_buf, "col", 7))
-    two_own = (one_float + total(d_buf, m)).astype(BF16)
-
-    two_buf[guide] = two_own
-    two_copies = spread(two_buf, "guide", 8)
-    own_float = two_own.astype(F32)
-    sq3_buf[guide, row] = squares(own_float)
-    sq_copies = []
-    for k in range(n):
-        targets = [{"row": peer("row", k), "guide": other}]
+    d_buf[guide, col] = down.astype(BF16)
+    d_copies = []
+    for k in range(m):
+        targets = [{"col": peer("col", k), "guide": other}]
         if k:
-            targets.append({"row": peer("row", k)})
+            targets.append({"col": peer("col", k)})
         for number, target in zip((0, 1), targets):
             copy = pltpu.make_async_remote_copy(
-                src_ref=sq3_buf.at[guide, row],
-                dst_ref=sq3_buf.at[guide, row],
-                send_sem=sq_sem.at[0, number, k],
-                recv_sem=sq_sem.at[1, number, k],
+                src_ref=d_buf.at[guide, col],
+                dst_ref=d_buf.at[guide, col],
+                send_sem=d_sem.at[0, number, k],
+                recv_sem=d_sem.at[1, number, k],
                 device_id=target,
                 device_id_type=MESH,
             )
             copy.start()
-            sq_copies.append(copy)
+            d_copies.append(copy)
+    finish(one_copies)
+    finish(d_copies)
+
+    twos = [
+        (one_buf[side].astype(F32) + total(d_buf.at[side], m)).astype(BF16).astype(F32)
+        for side in range(2)
+    ]
+    sq3_buf[row] = jnp.where(left, squares(twos[0]), squares(twos[1]))
+    sq_copies = spread(sq3_buf, "row", 9)
+    first = guide == 0
+    own_float = jnp.where(first, twos[0], twos[1])
     next_input = (own_float * next_gain_ref[...].astype(F32)[None, :]).astype(BF16)
     loads[6].wait()
     np_buf[row, :, 0:width_q] = mm(next_input, wnq[...]).astype(BF16)
     loads[7].wait()
     pairs_to(np_buf, next_input, wnkv)
-    finish(two_copies)
-    first = guide == 0
 
     def my_half(values):
         return jnp.where(first, values[:half_rows], values[half_rows:])
 
     both = jnp.concatenate(
-        [my_half(two_buf[0].astype(F32)), my_half(two_buf[1].astype(F32))], axis=0
+        [my_half(twos[0]), my_half(twos[1])], axis=0
     )
     np_copies = spread(np_buf, "row", 10)
     head_input = (both * final_gain_ref[...].astype(F32)[None, :]).astype(BF16)
@@ -416,10 +431,11 @@
             first_part[:, at : at + size] = raw(wh[pl.ds(start, size), :])
 
     finish(sq_copies)
-    sums = [total(sq3_buf.at[side], n) for side in range(2)]
-    own_scale = scale_of(jnp.where(first, sums[0], sums[1]))[:, 0:1]
-    factor_c = guidance * scale_of(my_half(sums[0]))[:, 0:1]
-    factor_u = (1.0 - guidance) * scale_of(my_half(sums[1]))[:, 0:1]
+    scales = scale_of(total(sq3_buf, n))
+    sides = [scales[:, 0:1], scales[:, HD : HD + 1]]
+    own_scale = jnp.where(first, sides[0], sides[1])
+    factor_c = guidance * my_half(sides[0])
+    factor_u = (1.0 - guidance) * my_half(sides[1])
 
     def blend(logits):
         return factor_c * logits[:half_rows] + factor_u * logits[half_rows:]
@@ -466,8 +482,7 @@
 
     finish(np_copies)
     sums = own_scale * total(np_buf, n)
-    nq_ref[...] = sums[:, :width_q].astype(BF16)
-    nkv_ref[...] = sums[:, width_q:].astype(BF16)
+    next_ref[...] = sums.astype(BF16)
 
     finish(copies)
     sums = total(h_buf, n)
@@ -488,6 +503,15 @@
             out_ref[:, j * LANES : j * LANES + wide] = joined[:, :wide]
     for copy in pending:
         copy.wait_send()
+
+
+def part_outputs(guided_ref, next_ref, out_ref, query_ref, pairs_ref):
+    out_ref[...] = guided_ref[...]
+    width_q = query_ref.shape[1]
+    width = pairs_ref.shape[2]
+    query_ref[...] = next_ref[:, 0:width_q]
+    for k in range(2):
+        pairs_ref[:, k, :] = next_ref[:, width_q + k * width : width_q + (k + 1) * width]
 
 
 def local(
@@ -536,6 +560,7 @@
     hbm = pl.BlockSpec(memory_space=pl.ANY)
     scratch = [pltpu.VMEM(a.shape, a.dtype) for a in weights] + [
         pltpu.VMEM((width, 2 * width), BF16),
+        pltpu.VMEM((2 * width, hidden_here), BF16),
         pltpu.VMEM((n, requests, width_q + width_kv), BF16),
         pltpu.VMEM((n, requests, LANES), F32),
         pltpu.VMEM((requests, heads_here, LANES), F32),
@@ -546,9 +571,9 @@
         pltpu.VMEM((n - 1 if scattered else 1, requests, gu_width), BF16),
         pltpu.VMEM((n, requests, gu_width), BF16),
         pltpu.VMEM((n, requests, block), BF16),
-        pltpu.VMEM((m, requests, width), BF16),
+        pltpu.VMEM((2, m, requests, width), BF16),
         pltpu.VMEM((2, requests, width), BF16),
-        pltpu.VMEM((2, n, requests, LANES), F32),
+        pltpu.VMEM((n, requests, LANES), F32),
         pltpu.VMEM((n, requests, width_q + width_kv), BF16),
         pltpu.VMEM(first_shape, F32),
         pltpu.VMEM(part_shape, F32),
@@ -557,24 +582,34 @@
         pltpu.SemaphoreType.DMA((8 + n,)),
         pltpu.SemaphoreType.DMA((14, peers)),
         pltpu.SemaphoreType.DMA((14, peers)),
-        pltpu.SemaphoreType.DMA((2, 2, n)),
+        pltpu.SemaphoreType.DMA((2, 2, m)),
     ]
-    guided, next_query, next_pairs = pl.pallas_call(
+    guided, next_all = pl.pallas_call(
         functools.partial(layer_kernel, n, m),
         out_shape=(
             jax.ShapeDtypeStruct((requests // 2, share), F32),
-            jax.ShapeDtypeStruct((requests, width_q), BF16),
-            jax.ShapeDtypeStruct((requests, width_kv), BF16),
+            jax.ShapeDtypeStruct((requests, width_q + width_kv), BF16),
         ),
         in_specs=[vmem, vmem, vmem, smem] + [vmem] * 4 + [hbm] * 9,
-        out_specs=(vmem, vmem, vmem),
+        out_specs=(vmem, vmem),
         scratch_shapes=scratch,
         compiler_params=pltpu.CompilerParams(
             collective_id=0, has_side_effects=True, vmem_limit_bytes=60 * 1024 * 1024
         ),
         name="decode_layer",
     )(x_rows, lengths, tenant.reshape(1, -1), guide_scale, attn_gain, mlp_gain, final_gain, next_gain, *weights)
-    return (guided, next_query[None], next_pairs.reshape(1, requests, 2, -1))
+    guided, next_query, next_pairs = pl.pallas_call(
+        part_outputs,
+        out_shape=(
+            jax.ShapeDtypeStruct(guided.shape, F32),
+            jax.ShapeDtypeStruct((requests, width_q), BF16),
+            jax.ShapeDtypeStruct((requests, 2, width_kv // 2), BF16),
+        ),
+        in_specs=[vmem, vmem],
+        out_specs=(vmem, vmem, vmem),
+        name="part_outputs",
+    )(guided, next_all)
+    return (guided, next_query[None], next_pairs[None])
 
 
 def solution(mesh):

time: 55.3 us -> 51.4 us (0.929)
  local copies, waits for them, and re-layouts: 4.29 us -> 0 us
    unnamed x2 -> x0, local copies, waits for them, and re-layouts: 2.98 us -> none
    pallas_call x1, Pallas kernels: 50 us -> 48.3 us  [local(): pl.pallas_call(functools.partial(layer_kernel, n, m), out_shape=(jax.Shap...]
    pallas_call x0 -> x1, Pallas kernels: none -> 1.67 us  [local(): pl.pallas_call(part_outputs, out_shape=(jax.ShapeDtypeStruct(guided.shape...]
    reshape x1 -> x0, local copies, waits for them, and re-layouts: 1.3 us -> none  [local(): return (guided, next_query[None], next_pairs.reshape(1, requests, 2, -1))]
where the time goes in v3:
time: 51.4 us; the launch traced here: 50.6 us
  Pallas kernels  49.9 us (97%)
  between operations  0.65 us (1%)
    pallas_call x1, Pallas kernels, local(): pl.pallas_call(functools.partial(layer_kernel, n, m), out_shape=(jax.Shap...  48.3 us
    pallas_call x1, Pallas kernels, local(): pl.pallas_call(part_outputs, out_shape=(jax.ShapeDtypeStruct(guided.shape...  1.67 us

profile of v3, /device:TPU:9, one launch (start us, length us, event | category | flops | bytes accessed | tf_op | source)
XLA Modules:
  0.0 50.6 jit_solution(10723567334545692799)
XLA Ops:
  0.6 48.3 %decode_layer.1 = (f32[8,8016]{1,0:T(8,128)}, bf16[16,768]{1,0:T(8,128)(2,1)}) custom-call(bf16[16,512]{1,0:T(8,128)(2,1)} %bitcast.8, s32[1,16]{1,0:T(1,128)} %len_ref.1, s32[1,16]{1,0:T(1,128)} %bitcast.9, f32[4]{0:T(128)} %guide_ref.1, bf16[512]{0:T(512)(128)(2,1)} %attn_gain_ref.1, bf16[512]{0:T(512)(128)(2,1)} %mlp_gain_ref.1, ...), custom_call_target="tpu_custom_call" | custom-call | tf_op jit(solution)/shard_map/decode_layer/pallas_call | solution.py:587
  48.9 1.7 %part_outputs.1 = (f32[8,8016]{1,0:T(8,128)}, bf16[16,512]{1,0:T(8,128)(2,1)}, bf16[16,2,128]{2,1,0:T(2,128)(2,1)}) custom-call(f32[8,8016]{1,0:T(8,128)} %get-tuple-element.8.guided_ref, bf16[16,768]{1,0:T(8,128)(2,1)} %get-tuple-element.9.next_ref), custom_call_target="tpu_custom_call" | custom-call | tf_op jit(solution)/shard_map/part_outputs/pallas_call | solution.py:601

commit v4 on v3

--- a/solution.py
+++ b/solution.py
@@ -91,6 +91,7 @@
     send_sem,
     recv_sem,
     d_sem,
+    h_sem,
 ):
     row = lax.axis_index("row")
     col = lax.axis_index("col")
@@ -110,8 +111,8 @@
     loads = [pltpu.make_async_copy(a, b, local_sem.at[i]) for i, (a, b) in enumerate(pairs)]
     for load in loads:
         load.start()
-    share = wh.shape[0] // n
-    exact = share % SUBLANES == 0
+    share = wh_hbm.shape[0] // n
+    exact = share % SUBLANES == 0 and window_of(share) % (8 * LANES) == 0
     if exact:
         head_loads = []
         for k in range(1, n + 1):
@@ -415,20 +416,44 @@
             head_input, rows, (((1,), (1,)), ((), ())), preferred_element_type=F32
         )
 
-    vocab = wh.shape[0]
+    vocab = share * n
     window = window_of(share)
     half = window // 2
-    chunk = 1024 if half % 1024 == 0 else half
+    chunk = window // 8 if exact else half
     whole = vocab // LANES * LANES
     last_start = (n - 1) * share // LANES * LANES
-    pieces = [(at, min(chunk, share - at)) for at in range(0, share, chunk)]
     copies = []
-    head_loads[0].wait()
+    for load in head_loads:
+        load.wait()
+    sub = 4 * chunk
+
+    def unit_rows(k, side, piece):
+        at = peer("row", k) * share + side * sub + piece * chunk
+        return wh[pl.ds(pl.multiple_of(at, SUBLANES), chunk), :]
+
+    def fold(values):
+        upper = jnp.concatenate(values[:2], axis=1)
+        lower = jnp.concatenate(values[2:], axis=1)
+        return jnp.concatenate([upper, lower], axis=0).astype(BF16)
+
+    def unit_copy(k, side):
+        return pltpu.make_async_remote_copy(
+            src_ref=h_send.at[2 * (k - 1) + side],
+            dst_ref=h_buf.at[row, side],
+            send_sem=h_sem.at[0, 2 * (k - 1) + side],
+            recv_sem=h_sem.at[1, 2 * (k - 1) + side],
+            device_id={"row": peer("row", k)},
+            device_id_type=MESH,
+        )
+
     if exact:
-        part[...] = jnp.zeros(part.shape, F32)
-        for at, size in pieces:
-            start = pl.multiple_of(peer("row", 1) * share + at, SUBLANES)
-            first_part[:, at : at + size] = raw(wh[pl.ds(start, size), :])
+
+        @pl.loop(0, 2)
+        def _(side):
+            for piece in range(4):
+                first_part[side, :, piece * chunk : (piece + 1) * chunk] = raw(
+                    unit_rows(1, side, piece)
+                )
 
     finish(sq_copies)
     scales = scale_of(total(sq3_buf, n))
@@ -443,26 +468,35 @@
     def guided(rows):
         return blend(raw(rows))
 
-    if not exact:
+    if exact:
+        for side in range(2):
+            values = [
+                blend(first_part[side, :, piece * chunk : (piece + 1) * chunk]) for piece in range(4)
+            ]
+            h_send[side] = fold(values)
+            unit_copy(1, side).start()
+
+        @pl.loop(2, 2 * n)
+        def _(unit):
+            k = 1 + unit // 2
+            side = unit % 2
+            folded = fold([guided(unit_rows(k, side, piece)) for piece in range(4)])
+
+            @pl.when(unit < 2 * (n - 1))
+            def _():
+                h_send[unit] = folded
+                unit_copy(k, side).start()
+
+            @pl.when(unit >= 2 * (n - 1))
+            def _():
+                h_buf[row, side] = folded
+
+    else:
         part[:, whole : part.shape[1]] = jnp.zeros((half_rows, part.shape[1] - whole), F32)
         if whole < vocab:
             part[:, whole:vocab] = guided(wh[whole:vocab, :])
-    for k in range(1, n + 1):
-        dest = peer("row", k)
-        if exact:
-            if k > 1:
-                head_loads[k - 1].wait()
-            for first_row, size in pieces:
-                at = pl.multiple_of(dest * share + first_row, SUBLANES)
-                top = first_row // half * half_rows
-                column = first_row % half
-                if k == 1:
-                    value = blend(first_part[:, first_row : first_row + size])
-                else:
-                    value = guided(wh[pl.ds(at, size), :])
-                part[top : top + half_rows, column : column + size] = value
-            stacked = part[...]
-        else:
+        for k in range(1, n + 1):
+            dest = peer("row", k)
             start = dest * share // LANES * LANES
             is_last = (dest + 1) // n
             for piece in range(window // chunk):
@@ -474,22 +508,34 @@
             stacked = jnp.concatenate(
                 [part[:, pl.ds(start, half)], part[:, pl.ds(upper, half)]], axis=0
             )
-        if k < n:
-            h_send[k - 1] = stacked.astype(BF16)
-            copies.append(send(h_send.at[k - 1], h_buf.at[row], "row", 11, k))
-        else:
-            h_buf[row] = stacked.astype(BF16)
+            if k < n:
+                h_send[k - 1] = stacked.astype(BF16)
+                copies.append(send(h_send.at[k - 1], h_buf.at[row], "row", 11, k))
+            else:
+                h_buf[row] = stacked.astype(BF16)
 
     finish(np_copies)
     sums = own_scale * total(np_buf, n)
     next_ref[...] = sums.astype(BF16)
 
-    finish(copies)
-    sums = total(h_buf, n)
     if exact:
-        out_ref[:, 0:half] = sums[:half_rows]
-        out_ref[:, half:share] = sums[half_rows:, 0 : share - half]
+        for side in range(2):
+            for k in range(1, n):
+                unit_copy(k, side).wait_recv()
+            sums = h_buf[0, side].astype(F32)
+            for k in range(1, n):
+                sums = sums + h_buf[k, side].astype(F32)
+            for quarter in range(2):
+                at = side * sub + quarter * 2 * chunk
+                wide = min(2 * chunk, share - at)
+                top = quarter * half_rows
+                out_ref[:, at : at + wide] = sums[top : top + half_rows, 0:wide]
+        for side in range(2):
+            for k in range(1, n):
+                unit_copy(k, side).wait_send()
     else:
+        finish(copies)
+        sums = total(h_buf, n)
         part[:, 0:half] = sums[:half_rows]
         part[:, half:window] = sums[half_rows:]
         offset = lax.rem(row * share, LANES)
@@ -549,16 +595,19 @@
     share = vocab // n
     window = window_of(share)
     last_start = (n - 1) * share // LANES * LANES
-    exact = share % SUBLANES == 0
-    part_shape = (requests, window // 2) if exact else (requests // 2, last_start + window)
-    first_shape = (requests, window) if exact else (requests, LANES)
+    exact = share % SUBLANES == 0 and window % (8 * LANES) == 0
+    part_shape = (8, LANES) if exact else (requests // 2, last_start + window)
+    held = [a.shape for a in weights]
+    if exact:
+        held[6] = (vocab + window - share, width)
+    first_shape = (2, requests, window // 2) if exact else (requests, LANES)
     scattered = block % LANES == 0
     gu_width = 2 * block if scattered else 2 * hidden_here
     peers = max(n, m) - 1
     vmem = pl.BlockSpec(memory_space=pltpu.VMEM)
     smem = pl.BlockSpec(memory_space=pltpu.SMEM)
     hbm = pl.BlockSpec(memory_space=pl.ANY)
-    scratch = [pltpu.VMEM(a.shape, a.dtype) for a in weights] + [
+    scratch = [pltpu.VMEM(shape, BF16) for shape in held] + [
         pltpu.VMEM((width, 2 * width), BF16),
         pltpu.VMEM((2 * width, hidden_here), BF16),
         pltpu.VMEM((n, requests, width_q + width_kv), BF16),
@@ -577,12 +626,13 @@
         pltpu.VMEM((n, requests, width_q + width_kv), BF16),
         pltpu.VMEM(first_shape, F32),
         pltpu.VMEM(part_shape, F32),
-        pltpu.VMEM((n - 1, requests, window // 2), BF16),
-        pltpu.VMEM((n, requests, window // 2), BF16),
+        pltpu.VMEM((2 * n - 2, requests, window // 4) if exact else (n - 1, requests, window // 2), BF16),
+        pltpu.VMEM((n, 2, requests, window // 4) if exact else (n, requests, window // 2), BF16),
         pltpu.SemaphoreType.DMA((8 + n,)),
         pltpu.SemaphoreType.DMA((14, peers)),
         pltpu.SemaphoreType.DMA((14, peers)),
         pltpu.SemaphoreType.DMA((2, 2, m)),
+        pltpu.SemaphoreType.DMA((2, 2 * n)),
     ]
     guided, next_all = pl.pallas_call(
         functools.partial(layer_kernel, n, m),

time: 51.4 us -> 51.6 us (level)
  Pallas kernels: 49.9 us -> 50.6 us
    pallas_call x1, Pallas kernels: 48.3 us -> 48.9 us  [local(): pl.pallas_call(functools.partial(layer_kernel, n, m), out_shape=(jax.Shap...]
where the time goes in v4:
time: 51.6 us; the launch traced here: 51.2 us
  Pallas kernels  50.6 us (98%)
  between operations  0.65 us (1%)
    pallas_call x1, Pallas kernels, local(): pl.pallas_call(functools.partial(layer_kernel, n, m), out_shape=(jax.Shap...  48.9 us
    pallas_call x1, Pallas kernels, local(): pl.pallas_call(part_outputs, out_shape=(jax.ShapeDtypeStruct(guided.shape...  1.67 us

profile of v4, /device:TPU:9, one launch (start us, length us, event | category | flops | bytes accessed | tf_op | source)
XLA Modules:
  0.0 51.2 jit_solution(5039085698535999475)
XLA Ops:
  0.6 48.9 %decode_layer.1 = (f32[8,8016]{1,0:T(8,128)}, bf16[16,768]{1,0:T(8,128)(2,1)}) custom-call(bf16[16,512]{1,0:T(8,128)(2,1)} %bitcast.8, s32[1,16]{1,0:T(1,128)} %len_ref.1, s32[1,16]{1,0:T(1,128)} %bitcast.9, f32[4]{0:T(128)} %guide_ref.1, bf16[512]{0:T(512)(128)(2,1)} %attn_gain_ref.1, bf16[512]{0:T(512)(128)(2,1)} %mlp_gain_ref.1, ...), custom_call_target="tpu_custom_call" | custom-call | tf_op jit(solution)/shard_map/decode_layer/pallas_call | solution.py:637
  49.6 1.7 %part_outputs.1 = (f32[8,8016]{1,0:T(8,128)}, bf16[16,512]{1,0:T(8,128)(2,1)}, bf16[16,2,128]{2,1,0:T(2,128)(2,1)}) custom-call(f32[8,8016]{1,0:T(8,128)} %get-tuple-element.8.guided_ref, bf16[16,768]{1,0:T(8,128)(2,1)} %get-tuple-element.9.next_ref), custom_call_target="tpu_custom_call" | custom-call | tf_op jit(solution)/shard_map/part_outputs/pallas_call | solution.py:651
